TPU v7x, 32 devices: a whole 2x2x4 slice. The times are simulated.
32 devices in a mesh: groups: 2 (over y), ep: 8 (over z, x), hg: 2 (over core).
Axes of the slice: x: 2, y: 2, z: 4, core: 2. Of those that a mesh axis runs over, the one named last changes fastest.
Arguments:
- tokens: bfloat16 [64, 3584], P(('groups', 'ep')), parts along dimension 0, may hold values from -6 to 6
- norm_gain: float32 [3584], replicated, may hold values from 0.1 to 1.9
- route_scores: float32 [64, 8], P(('groups', 'ep')), parts along dimension 0, may hold values from 0.02 to 1
- expert_ids: int32 [64, 8], P(('groups', 'ep')), parts along dimension 0, may hold values from 0 to 15, all different within a row; in each aligned block of 2 rows (0 to 1, 2 to 3, ...) at most 2 rows name the same one
- gate_weight: bfloat16 [3584, 32768], P(None, ('ep', 'hg')), may hold values from -0.09375 to 0.09375
- up_weight: bfloat16 [3584, 32768], P(None, ('ep', 'hg')), may hold values from -0.09375 to 0.09375
- down_weight: bfloat16 [32768, 3584], P(('ep', 'hg')), may hold values from -0.125 to 0.125
Outputs:
- mixed: bfloat16 [64, 3584], P(('groups', 'ep'), 'hg'), parts along dimension 0
There are 2 independent parts, one for each index of `groups`. A program takes and returns all parts, laid end to end along the dimension named above; an argument that names none is the same for every part. Nothing has to cross between parts.
Inputs may be any that keep to these rules, and one draw needn't show every extreme that they name: `expert_ids`: each token names 8 different experts. Token rows are laid out by ep index, then micro-batch, then row; in each micro-batch of one ep index (aligned blocks of 2 rows) no expert is named by more than 2 tokens, and in every draw some expert is named by exactly 2 tokens of some block.
All inputs are finite; a program needn't handle non-finite values.
Results may differ from a plain program's by a relative error of at most 0.0055.
Values may be sent and summed in bfloat16 or wider, within the bound.
A program may use at most 128 MiB of HBM per device.

v0:
```python
import jax
import jax.numpy as jnp
from jax import lax
from jax.sharding import PartitionSpec as P

FF = 2048
EXPERTS = 16
TOP = 8
MICRO = 2
ROWS = 2
CAP = 2


ROUTE_SCALE = 2.5
NORM_EPS = 1e-06


def route_onehots(chosen_ids):
    chosen = (chosen_ids[..., None] == jnp.arange(EXPERTS, dtype=jnp.int32)).astype(jnp.int32)
    blocks = chosen_ids.shape[0]
    flat = chosen.reshape(blocks, ROWS * TOP, EXPERTS)
    earlier = jnp.cumsum(flat, axis=1) - flat
    position = jnp.sum(earlier * flat, axis=2).reshape(blocks, ROWS, TOP)
    placed = (position[..., None] == jnp.arange(CAP, dtype=jnp.int32)).astype(jnp.float32)
    return (chosen.astype(jnp.float32), placed)


def dispatch_table(chosen_ids):
    chosen, placed = route_onehots(chosen_ids)
    return jnp.einsum("brte,brtc->becr", chosen, placed)


def combine_table(chosen_ids, weights):
    chosen, placed = route_onehots(chosen_ids)
    return jnp.einsum(
        "brte,brtc,brt->becr", chosen, placed, weights, precision=lax.Precision.HIGHEST
    )


def body(tokens, norm_gain, route_scores, expert_ids, gate_weight, up_weight, down_weight):
    n_ep = lax.axis_size("ep")
    n_hg = lax.axis_size("hg")
    width = tokens.shape[1]
    shard = gate_weight.shape[1]
    block = min(shard, FF)
    local = shard // block
    lane = lax.axis_index("hg")
    stats = tokens.astype(jnp.float32)
    scale = lax.rsqrt(jnp.mean(stats * stats, axis=1, keepdims=True) + NORM_EPS)
    normed = (stats * scale * norm_gain[None, :]).astype(jnp.bfloat16)
    weights = ROUTE_SCALE * route_scores / jnp.sum(route_scores, axis=1, keepdims=True)
    own_ids = expert_ids.reshape(MICRO, ROWS, TOP)
    combine = combine_table(own_ids, weights.reshape(MICRO, ROWS, TOP))
    holders = jnp.arange(n_ep, dtype=jnp.int32)[None, :]
    owners = (holders * n_hg + lane) * shard // FF + jnp.arange(local, dtype=jnp.int32)[:, None]
    dispatch = dispatch_table(own_ids).astype(jnp.bfloat16)
    slotted = jnp.einsum(
        "mecr,mrd->emcd",
        dispatch,
        normed.reshape(MICRO, ROWS, width),
        preferred_element_type=jnp.float32,
    ).astype(jnp.bfloat16)
    outgoing = jnp.take(slotted, owners.reshape(-1), axis=0).reshape(local, n_ep, MICRO, CAP, width)
    arrived = lax.all_to_all(outgoing, "ep", split_axis=1, concat_axis=1, tiled=True)
    rows_in = arrived.reshape(local, n_ep * MICRO * CAP, width)
    gate_val = jnp.einsum(
        "lnd,dlf->lnf",
        rows_in,
        gate_weight.reshape(width, local, block),
        preferred_element_type=jnp.float32,
    )
    up_val = jnp.einsum(
        "lnd,dlf->lnf",
        rows_in,
        up_weight.reshape(width, local, block),
        preferred_element_type=jnp.float32,
    )
    act = (jax.nn.silu(gate_val) * up_val).astype(jnp.bfloat16)
    partial_value = jnp.einsum(
        "lnf,lfd->lnd",
        act,
        down_weight.reshape(local, block, width),
        preferred_element_type=jnp.float32,
    ).astype(jnp.bfloat16)
    returned = lax.all_to_all(
        partial_value.reshape(local, n_ep, MICRO, CAP, width),
        "ep",
        split_axis=1,
        concat_axis=1,
        tiled=True,
    )
    select = (owners.reshape(-1)[:, None] == jnp.arange(EXPERTS, dtype=jnp.int32)[None, :]).astype(
        jnp.bfloat16
    )
    collected = jnp.einsum(
        "ke,kmcd->emcd",
        select,
        returned.reshape(local * n_ep, MICRO, CAP, width),
        preferred_element_type=jnp.float32,
    )
    moe_part = jnp.einsum(
        "mecr,emcd->mrd", combine, collected, precision=lax.Precision.HIGHEST
    ).reshape(MICRO * ROWS, width)
    summed = lax.psum_scatter(moe_part, "hg", scatter_dimension=1, tiled=True)
    half = width // n_hg
    resid = lax.dynamic_slice_in_dim(stats, lane * half, half, 1)
    return (resid + summed).astype(jnp.bfloat16)


def solution(mesh):
    return jax.shard_map(
        body,
        mesh=mesh,
        in_specs=(
            P(("groups", "ep"), None),
            P(),
            P(("groups", "ep"), None),
            P(("groups", "ep"), None),
            P(None, ("ep", "hg")),
            P(None, ("ep", "hg")),
            P(("ep", "hg"), None),
        ),
        out_specs=P(("groups", "ep"), "hg"),
        check_vma=False,
    )
```

profile of v0, /device:TPU:0, one launch (start us, length us, event | category | flops | bytes accessed | tf_op | source)
XLA Modules:
  0.0 83.7 jit_solution(13600484575359927981)
XLA Ops:
  6.6 0.8 eq.31
  7.3 0.1 fusion.18
  7.4 0.2 select_reduce_fusion
  7.6 0.1 eq.70
  7.7 0.9 %multiply_reduce_fusion = f32[4]{0:T(128)S(1)} fusion(bf16[4,3584]{1,0:T(4,128)(2,1)} %param.7), kind=kLoop, calls=%fused_computation.22 | loop fusion | flops 43004 | bytes 28688 | tf_op jit(solution)/shard_map/reduce_sum | solution.py:49
  8.6 0.9 %multiply_convert_fusion = bf16[4,3584]{1,0:T(4,128)(2,1)S(1)} fusion(f32[3584]{0:T(1024)} %param.8, f32[4]{0:T(128)S(1)} %add_rsqrt_fusion, bf16[4,3584]{1,0:T(4,128)(2,1)} %param.7), kind=kLoop, calls=%fused_computation.21 | loop fusion | flops 57344 | bytes 71696 | tf_op jit(solution)/shard_map/convert_element_type | solution.py:50
  9.5 0.9 %fusion.2 = bf16[2,16,2,2]{1,2,3,0:T(2,128)(2,1)S(1)} fusion(s32[2,2,8]{2,1,0:T(2,128)} %bitcast.43, s32[2,2,8]{2,1,0:T(2,128)S(1)} %eq.70), kind=kOutput, calls=%fused_computation.9 | convolution fusion | flops 3776 | bytes 512 | tf_op jit(solution)/shard_map/brte,brtc->becr/dot_general | solution.py:30
  10.4 0.3 fusion
  10.7 0.5 copy.10
  11.2 1.0 %gather_fusion = bf16[8,2,2,3584]{3,2,1,0:T(2,128)(2,1)S(1)} fusion(bf16[16,2,2,3584]{3,2,1,0:T(2,128)(2,1)S(1)} %copy.10, s32[1024]{0:T(1024)S(1)} %pad_clamp_fusion), kind=kCustom, calls=%fused_computation | custom fusion | bytes 458784 | tf_op jit(solution)/shard_map/jit(_take)/gather | solution.py:63
  12.2 0.9 %fusion.11 = bf16[1,8,2,2,3584]{4,3,2,0,1:T(2,128)(2,1)} fusion(bf16[8,2,2,3584]{3,2,1,0:T(2,128)(2,1)S(1)} %gather_fusion, pred[8]{0:T(512)(128)(4,1)S(1)} %compare_and_fusion), kind=kLoop, calls=%fused_computation.19 | loop fusion | flops 114688 | bytes 458760 | tf_op jit(solution)/shard_map/jit(_take)/select_n | solution.py:63
  13.2 7.2 %all-to-all-start = ((bf16[1,8,2,2,3584]{4,3,2,0,1:T(2,128)(2,1)}), bf16[1,8,2,2,3584]{4,3,2,0,1:T(2,128)(2,1)S(1)}, u32[]{:S(2)}, u32[]{:S(2)}) async-start(bf16[1,8,2,2,3584]{4,3,2,0,1:T(2,128)(2,1)} %fusion.11), calls=%async_computation | async-start | bytes 458752 | tf_op jit(solution)/shard_map/all_to_all | solution.py:64
  20.4 0.8 reduce_sum.32
  21.2 7.6 %all-to-all-done = bf16[1,8,2,2,3584]{4,3,2,0,1:T(2,128)(2,1)S(1)} async-done(((bf16[1,8,2,2,3584]{4,3,2,0,1:T(2,128)(2,1)}), bf16[1,8,2,2,3584]{4,3,2,0,1:T(2,128)(2,1)S(1)}, u32[]{:S(2)}, u32[]{:S(2)}) %all-to-all-start) | async-done | bytes 229408 | tf_op jit(solution)/shard_map/all_to_all | solution.py:64
  28.8 0.1 reshape.170
  28.9 7.8 %fusion.34 = f32[32,2048]{1,0:T(8,128)S(1)} fusion(bf16[32,3584]{1,0:T(8,128)(2,1)S(1)} %reshape.170, bf16[3584,2048]{1,0:T(8,128)(2,1)} %param.11), kind=kOutput, calls=%fused_computation.63 | convolution fusion | flops 469762048 | bytes 15171584 | tf_op jit(solution)/shard_map/lnd,dlf->lnf/dot_general | solution.py:66
  36.7 0.0 copy-start.1
  36.7 0.0 copy-start.2
  36.7 0.0 copy-start
  36.8 14.5 %convolution_convert_fusion.1 = bf16[32,3584]{1,0:T(8,128)(2,1)S(1)} fusion(bf16[2048,3584]{1,0:T(8,128)(2,1)} %param.13, bf16[32,3584]{1,0:T(8,128)(2,1)S(1)} %reshape.170, bf16[3584,2048]{1,0:T(8,128)(2,1)} %param.12, f32[32,2048]{1,0:T(8,128)S(1)} %fusion.34), kind=kOutput, calls=%fused_computation.3 | convolution fusion | flops 940032000 | bytes 30081024 | tf_op jit(solution)/shard_map/lnf,lfd->lnd/dot_general | solution.py:79
  51.3 0.8 reshape.171
  52.1 3.4 %all-to-all-start.1 = ((bf16[1,8,2,2,3584]{4,3,2,0,1:T(2,128)(2,1)}), bf16[1,8,2,2,3584]{4,3,2,0,1:T(2,128)(2,1)S(1)}, u32[]{:S(2)}, u32[]{:S(2)}) async-start(bf16[1,8,2,2,3584]{4,3,2,0,1:T(2,128)(2,1)} %bitcast.11), calls=%async_computation.1 | async-start | bytes 458752 | tf_op jit(solution)/shard_map/all_to_all | solution.py:85
  55.5 0.0 reduce-scatter.4.cloned.1.call-start
  55.5 0.0 copy-done.1
  55.5 0.1 multiply_divide_fusion
  55.6 0.0 copy-done.2
  55.6 0.2 convolution_bitcast_fusion.1
  55.8 7.7 %all-to-all-done.1 = bf16[1,8,2,2,3584]{4,3,2,0,1:T(2,128)(2,1)S(1)} async-done(((bf16[1,8,2,2,3584]{4,3,2,0,1:T(2,128)(2,1)}), bf16[1,8,2,2,3584]{4,3,2,0,1:T(2,128)(2,1)S(1)}, u32[]{:S(2)}, u32[]{:S(2)}) %all-to-all-start.1) | async-done | bytes 229408 | tf_op jit(solution)/shard_map/all_to_all | solution.py:85
  63.6 0.4 fusion.8
  64.0 0.6 convolution_bitcast_fusion
  64.6 0.1 reshape.173
  64.6 1.8 %copy.18 = f32[4,3584]{0,1:T(8,128)} copy(f32[4,3584]{1,0:T(4,128)S(1)} %reshape.173) | data formatting | bytes 114688
  66.5 0.0 reduce-scatter.4.cloned.1.call-update
  66.5 0.0 copy-done
  66.5 8.3 %reduce-scatter.4.cloned.1.call-done = f32[1792,4]{1,0:T(8,128)} async-done(((f32[3584,4]{1,0:T(8,128)}), f32[1792,4]{1,0:T(8,128)}) %reduce-scatter.4.cloned.1.call-update) | async-done | bytes 28688
  74.8 1.5 %copy.19 = f32[4,1792]{1,0:T(4,128)S(1)} copy(f32[4,1792]{0,1:T(8,128)} %bitcast.42) | data formatting | bytes 57344
  76.3 0.6 add_convert_fusion
  (8 shorter events, 0.1 us)
Async XLA Ops:
  13.2 15.7 %all-to-all-start = ((bf16[1,8,2,2,3584]{4,3,2,0,1:T(2,128)(2,1)}), bf16[1,8,2,2,3584]{4,3,2,0,1:T(2,128)(2,1)S(1)}, u32[]{:S(2)}, u32[]{:S(2)}) async-start(bf16[1,8,2,2,3584]{4,3,2,0,1:T(2,128)(2,1)} %fusion.11), calls=%async_computation | async-start | bytes 458752 | tf_op jit(solution)/shard_map/all_to_all | solution.py:64
  36.7 18.8 %copy-start.1 = (f32[4,8]{1,0:T(4,128)S(1)}, f32[4,8]{1,0:T(4,128)}, u32[]{:S(2)}) copy-start(f32[4,8]{1,0:T(4,128)} %param.9) | copy-start | bytes 388
  36.7 18.9 %copy-start.2 = (s32[4,8]{1,0:T(4,128)S(1)}, s32[4,8]{1,0:T(4,128)}, u32[]{:S(2)}) copy-start(s32[4,8]{1,0:T(4,128)} %param.10) | copy-start | bytes 388
  36.7 29.7 %copy-start = (bf16[4,3584]{1,0:T(4,128)(2,1)S(1)}, bf16[4,3584]{1,0:T(4,128)(2,1)}, u32[]{:S(2)}) copy-start(bf16[4,3584]{1,0:T(4,128)(2,1)} %param.7) | copy-start | bytes 86020
  52.1 11.5 %all-to-all-start.1 = ((bf16[1,8,2,2,3584]{4,3,2,0,1:T(2,128)(2,1)}), bf16[1,8,2,2,3584]{4,3,2,0,1:T(2,128)(2,1)S(1)}, u32[]{:S(2)}, u32[]{:S(2)}) async-start(bf16[1,8,2,2,3584]{4,3,2,0,1:T(2,128)(2,1)} %bitcast.11), calls=%async_computation.1 | async-start | bytes 458752 | tf_op jit(solution)/shard_map/all_to_all | solution.py:85
  55.5 19.3 %reduce-scatter.4.cloned.1.call-start = ((), (), s32[]{:S(2)}) async-start(), calls=%async_computation.3 | async-start | bytes 2752512
Sparse Core Ops, SparseCore 0:
  66.6 8.1 reduce-scatter.3
where the time goes:
time: 84.3 us; the launch traced here: 83.7 us
  matrix products  24.7 us (29%)
  waiting for transfers between devices  23.7 us (28%)
  between operations  13.5 us (16%)
  starting transfers between devices  10.7 us (13%)
  local copies, waits for them, and re-layouts  6.59 us (8%)
  other arithmetic  4.55 us (5%)
    dot_general x1, matrix products, body(): jnp.einsum('lnf,lfd->lnd', act, down_weight.reshape(local, block, width),...  14.5 us
    unnamed x2, waiting for transfers between devices  8.32 us
    dot_general x1, matrix products, body(): jnp.einsum('lnd,dlf->lnf', rows_in, gate_weight.reshape(width, local, blo...  7.79 us
    all_to_all x1, waiting for transfers between devices, body(): lax.all_to_all(partial_value.reshape(local, n_ep, MICRO, CAP, width), 'ep...  7.73 us
    all_to_all x1, waiting for transfers between devices, body(): lax.all_to_all(outgoing, 'ep', split_axis=1, concat_axis=1, tiled=True)  7.62 us
    all_to_all x1, starting transfers between devices, body(): lax.all_to_all(outgoing, 'ep', split_axis=1, concat_axis=1, tiled=True)  7.25 us
    all_to_all x1, starting transfers between devices, body(): lax.all_to_all(partial_value.reshape(local, n_ep, MICRO, CAP, width), 'ep...  3.4 us
    unnamed x8, local copies, waits for them, and re-layouts  3.33 us
  transfers between devices with their start and end apart: 3, of which 3 were waited for; matrix products, arithmetic and copies ran while one was open for 1% of the time, Pallas kernels for 0%

commit v1 on v0

v1 whole, which is shorter than its diff:
```python
import functools
import jax
import jax.numpy as jnp
from jax import lax
from jax.experimental import pallas as pl
from jax.experimental.pallas import tpu as pltpu
from jax.sharding import PartitionSpec as P

FF = 2048
ROUTE_SCALE = 2.5
NORM_EPS = 1e-06
MESH = pl.DeviceIdType.MESH


def loop(count, step):
    if count == 1:
        step(0)
        return

    def once(i, carry):
        step(i)
        return carry

    lax.fori_loop(0, count, once, 0)


def kernel(
    n_ep,
    n_hg,
    tokens_ref,
    gain_ref,
    scores_ref,
    ids_ref,
    gate_ref,
    up_ref,
    down_ref,
    out_ref,
    gathered,
    gain,
    normed,
    gate_buf,
    up_buf,
    act,
    down_buf,
    outgoing,
    incoming,
    coef,
    gate_sem,
    up_sem,
    down_sem,
    gain_sem,
    token_send,
    token_recv,
    part_send,
    part_recv,
):
    group = lax.axis_index("groups")
    me = lax.axis_index("ep")
    lane = lax.axis_index("hg")
    rows, width = tokens_ref.shape
    chunks, _, chunk = gate_buf.shape
    shard = chunks * chunk
    half = width // n_hg
    pieces, _, _, _, piece = outgoing.shape
    parts = pieces * n_hg

    def gate_copy(c):
        cols = pl.ds(pl.multiple_of(c * chunk, 128), chunk)
        return pltpu.make_async_copy(gate_ref.at[:, cols], gate_buf.at[c], gate_sem.at[c])

    def up_copy(c):
        cols = pl.ds(pl.multiple_of(c * chunk, 128), chunk)
        return pltpu.make_async_copy(up_ref.at[:, cols], up_buf.at[c], up_sem.at[c])

    def down_copy(q):
        side = (lane + n_hg - 1 - q % n_hg) % n_hg
        start = side * half + q // n_hg * piece
        cols = pl.ds(pl.multiple_of(start, 128), piece)
        return pltpu.make_async_copy(down_ref.at[:, cols], down_buf.at[q], down_sem.at[q])

    def start_in(c):
        gate_copy(c).start()
        up_copy(c).start()

    own = pltpu.make_async_copy(tokens_ref, gathered.at[me], token_recv)
    own.start()
    gain_copy = pltpu.make_async_copy(gain_ref, gain, gain_sem)
    gain_copy.start()
    loop(chunks, start_in)

    barrier = pltpu.get_barrier_semaphore()
    for r in range(n_hg):
        side = (lane + r) % n_hg

        def greet(d):
            peer = (me + d + (r == 0)) % n_ep
            pl.semaphore_signal(barrier, inc=1, device_id=(group, peer, side), device_id_type=MESH)

        loop(n_ep - (r == 0), greet)
    pl.semaphore_wait(barrier, n_ep * n_hg - 1)

    def send_tokens(d):
        pltpu.make_async_remote_copy(
            src_ref=tokens_ref,
            dst_ref=gathered.at[me],
            send_sem=token_send,
            recv_sem=token_recv,
            device_id=(group, (me + d + 1) % n_ep, lane),
            device_id_type=MESH,
        ).start()

    loop(n_ep - 1, send_tokens)
    loop(parts, lambda q: down_copy(q).start())

    scores = scores_ref[...]
    weights = ROUTE_SCALE * scores / jnp.sum(scores, axis=1, keepdims=True)
    chosen = ids_ref[...]

    def weigh(s):
        expert = s * shard // FF
        total = jnp.sum(jnp.where(chosen == expert, weights, 0.0), axis=1, keepdims=True)
        coef[s] = jnp.broadcast_to(total, (rows, 128))

    loop(n_ep * n_hg, weigh)

    gain_copy.wait()
    pltpu.make_async_copy(gathered, gathered, token_recv).wait()
    batch = 16 // rows

    def norm(i):
        stats = jnp.concatenate(
            [gathered[i * batch + b].astype(jnp.float32) for b in range(batch)], axis=0
        )
        scale = lax.rsqrt(jnp.mean(stats * stats, axis=1, keepdims=True) + NORM_EPS)
        rows_at = pl.ds(pl.multiple_of(i * 16, 16), 16)
        normed[rows_at, :] = (stats * scale * gain[...]).astype(jnp.bfloat16)

    loop(n_ep // batch, norm)

    def first(c):
        gate_copy(c).wait()
        up_copy(c).wait()
        gate_val = jnp.dot(normed[...], gate_buf[c], preferred_element_type=jnp.float32)
        up_val = jnp.dot(normed[...], up_buf[c], preferred_element_type=jnp.float32)
        value = gate_val / (1.0 + jnp.exp(-gate_val)) * up_val
        act[:, pl.ds(pl.multiple_of(c * chunk, 128), chunk)] = value.astype(jnp.bfloat16)

    loop(chunks, first)

    source = me * n_hg + lane

    def second(p):
        for r in reversed(range(n_hg)):
            side = (lane + r) % n_hg
            q = p * n_hg + n_hg - 1 - r
            down_copy(q).wait()
            value = jnp.dot(act[...], down_buf[q], preferred_element_type=jnp.float32)
            for j in range(n_ep):
                outgoing[p, r, j] = value[j * rows : (j + 1) * rows].astype(jnp.bfloat16)

            def send(d):
                peer = (me + d + (r == 0)) % n_ep
                pltpu.make_async_remote_copy(
                    src_ref=outgoing.at[p, r, peer],
                    dst_ref=incoming.at[p, source],
                    send_sem=part_send.at[p, r],
                    recv_sem=part_recv.at[p],
                    device_id=(group, peer, side),
                    device_id_type=MESH,
                ).start()

            loop(n_ep - (r == 0), send)
            if r == 0:
                pltpu.make_async_copy(
                    outgoing.at[p, r, me], incoming.at[p, source], part_recv.at[p]
                ).start()

    loop(pieces, second)

    def finish(p):
        here = incoming.at[p]
        pltpu.make_async_copy(here, here, part_recv.at[p]).wait()
        start = pl.multiple_of(lane * half + p * piece, 128)
        resid = gathered[me, :, pl.ds(start, piece)].astype(jnp.float32)

        def add(s, total):
            weight = jnp.concatenate([coef[s]] * (piece // 128), axis=1)
            return total + weight * incoming[p, s].astype(jnp.float32)

        moe = lax.fori_loop(
            0, n_ep * n_hg, add, jnp.zeros((rows, piece), jnp.float32), unroll=min(16, n_ep * n_hg)
        )
        cols = pl.ds(pl.multiple_of(p * piece, 128), piece)
        out_ref[:, cols] = (resid + moe).astype(jnp.bfloat16)

    loop(pieces, finish)

    rest = gathered.at[pl.ds(0, n_ep - 1)]
    pltpu.make_async_copy(rest, rest, token_send).wait()

    def drain(p):
        for r in range(n_hg):
            sent = outgoing.at[p, r, pl.ds(0, n_ep - (r == 0))]
            pltpu.make_async_copy(sent, sent, part_send.at[p, r]).wait()

    loop(pieces, drain)


def body(tokens, norm_gain, route_scores, expert_ids, gate_weight, up_weight, down_weight):
    n_ep = lax.axis_size("ep")
    n_hg = lax.axis_size("hg")
    rows, width = tokens.shape
    shard = gate_weight.shape[1]
    chunk = min(shard, 256)
    chunks = shard // chunk
    half = width // n_hg
    piece = 256
    pieces = half // piece
    total = rows * n_ep
    sources = n_ep * n_hg
    hbm = pl.BlockSpec(memory_space=pl.ANY)
    vmem = pl.BlockSpec(memory_space=pltpu.VMEM)
    dma = pltpu.SemaphoreType.DMA
    return pl.pallas_call(
        functools.partial(kernel, n_ep, n_hg),
        out_shape=jax.ShapeDtypeStruct((rows, half), jnp.bfloat16),
        in_specs=[hbm, hbm, vmem, vmem, hbm, hbm, hbm],
        out_specs=vmem,
        scratch_shapes=[
            pltpu.VMEM((n_ep, rows, width), jnp.bfloat16),
            pltpu.VMEM((1, width), jnp.float32),
            pltpu.VMEM((total, width), jnp.bfloat16),
            pltpu.VMEM((chunks, width, chunk), jnp.bfloat16),
            pltpu.VMEM((chunks, width, chunk), jnp.bfloat16),
            pltpu.VMEM((total, shard), jnp.bfloat16),
            pltpu.VMEM((pieces * n_hg, shard, piece), jnp.bfloat16),
            pltpu.VMEM((pieces, n_hg, n_ep, rows, piece), jnp.bfloat16),
            pltpu.VMEM((pieces, sources, rows, piece), jnp.bfloat16),
            pltpu.VMEM((sources, rows, 128), jnp.float32),
            dma((chunks,)),
            dma((chunks,)),
            dma((pieces * n_hg,)),
            dma,
            dma,
            dma,
            dma((pieces, n_hg)),
            dma((pieces,)),
        ],
        compiler_params=pltpu.CompilerParams(
            collective_id=0, has_side_effects=True, vmem_limit_bytes=56 * 1024 * 1024
        ),
    )(
        tokens,
        norm_gain.reshape(1, width),
        route_scores,
        expert_ids,
        gate_weight,
        up_weight,
        down_weight,
    )


def solution(mesh):
    return jax.shard_map(
        body,
        mesh=mesh,
        in_specs=(
            P(("groups", "ep"), None),
            P(),
            P(("groups", "ep"), None),
            P(("groups", "ep"), None),
            P(None, ("ep", "hg")),
            P(None, ("ep", "hg")),
            P(("ep", "hg"), None),
        ),
        out_specs=P(("groups", "ep"), "hg"),
        check_vma=False,
    )
```

time: 84.3 us -> 34.9 us (0.41)
  Pallas kernels: 0 us -> 31.9 us
  matrix products: 24.7 us -> 0 us
  waiting for transfers between devices: 23.7 us -> 0 us
  between operations: 13.5 us -> 0.01 us
  starting transfers between devices: 10.7 us -> 0 us
  other arithmetic: 4.55 us -> 0 us
  local copies, waits for them, and re-layouts: 6.59 us -> 2.65 us
    pallas_call x0 -> x1, Pallas kernels: none -> 31.9 us  [body(): pl.pallas_call(functools.partial(kernel, n_ep, n_hg), out_shape=jax.Shape...]
    dot_general x7 -> x0, matrix products: 24.7 us -> none  [the longest x1 14.5 us: body(): jnp.einsum('lnf,lfd->lnd', act, down_weight.reshape(local, block, width),...]
    all_to_all x2 -> x0, waiting for transfers between devices: 15.4 us -> none  [the longest x1 7.73 us: body(): lax.all_to_all(partial_value.reshape(local, n_ep, MICRO, CAP, width), 'ep...]
    all_to_all x2 -> x0, starting transfers between devices: 10.6 us -> none  [the longest x1 7.25 us: body(): lax.all_to_all(outgoing, 'ep', split_axis=1, concat_axis=1, tiled=True)]
    unnamed x2 -> x0, waiting for transfers between devices: 8.32 us -> none
    unnamed x8 -> x1, local copies, waits for them, and re-layouts: 3.33 us -> 1.32 us
    reduce_sum x3 -> x0, other arithmetic: 1.88 us -> none  [the longest x1 0.9 us: body(): scale = lax.rsqrt(jnp.mean(stats * stats, axis=1, keepdims=True) + NORM_EPS)]
    convert_element_type x4 -> x0, other arithmetic: 1.56 us -> none  [the longest x1 0.85 us: body(): normed = (stats * scale * norm_gain[None, :]).astype(jnp.bfloat16)]
  transfers between devices with their start and end apart: 3 -> 0, of which waited for: 3 -> 0; matrix products, arithmetic and copies ran while one was open for 1% -> 0% of each run, Pallas kernels for 0% -> 0%
where the time goes in v1:
time: 34.9 us; the launch traced here: 34.5 us
  Pallas kernels  31.9 us (91%)
  local copies, waits for them, and re-layouts  2.65 us (8%)
    pallas_call x1, Pallas kernels, body(): pl.pallas_call(functools.partial(kernel, n_ep, n_hg), out_shape=jax.Shape...  31.9 us
    reshape x1, local copies, waits for them, and re-layouts, body(): norm_gain.reshape(1, width)  1.33 us
    unnamed x1, local copies, waits for them, and re-layouts  1.32 us

profile of v1, /device:TPU:0, one launch (start us, length us, event | category | flops | bytes accessed | tf_op | source)
XLA Modules:
  0.0 34.5 jit_solution(16187561101551179576)
XLA Ops:
  0.0 1.3 %reshape.3.gain_ref = f32[1,3584]{1,0:T(1,128)} reshape(f32[3584]{0:T(1024)} %param.8) | data formatting | bytes 28672 | tf_op jit(solution)/shard_map/reshape | solution.py:254
  1.3 31.9 %shard_map.73 = bf16[4,1792]{1,0:T(4,128)(2,1)} custom-call(bf16[4,3584]{1,0:T(4,128)(2,1)} %tokens_ref.1, f32[1,3584]{1,0:T(1,128)} %reshape.3.gain_ref, f32[4,8]{1,0:T(4,128)} %scores_ref.1, s32[4,8]{1,0:T(4,128)} %ids_ref.1, bf16[3584,2048]{1,0:T(8,128)(2,1)} %gate_ref.1, bf16[3584,2048]{1,0:T(8,128)(2,1)} %up_ref.1, bf16[2048,3584]{1,0:T(8,128)(2,1)} %down_ref.1), custom_call_target="tpu_custom_call" | custom-call | tf_op jit(solution)/shard_map/pallas_call | solution.py:224
  33.2 1.3 %copy.9 = bf16[4,1792]{1,0:T(4,128)(2,1)} copy(bf16[4,1792]{1,0:T(4,128)(2,1)} %shard_map.73) | data formatting | bytes 28672

commit v2 on v1

v2 whole, which is shorter than its diff:
```python
import functools
import jax
import jax.numpy as jnp
from jax import lax
from jax.experimental import pallas as pl
from jax.experimental.pallas import tpu as pltpu
from jax.sharding import PartitionSpec as P

FF = 2048
ROUTE_SCALE = 2.5
NORM_EPS = 1e-06
MESH = pl.DeviceIdType.MESH


def loop(count, step):
    if count == 1:
        step(0)
        return

    def once(i, carry):
        step(i)
        return carry

    lax.fori_loop(0, count, once, 0)


def kernel(
    n_ep,
    n_hg,
    tokens_ref,
    gain_ref,
    scores_ref,
    ids_ref,
    gate_ref,
    up_ref,
    down_ref,
    out_ref,
    tokens,
    gain,
    gathered,
    normed,
    gate_buf,
    up_buf,
    gate_sum,
    up_sum,
    act,
    down_buf,
    outgoing,
    incoming,
    coef,
    gate_sem,
    up_sem,
    down_sem,
    own_sem,
    row_send,
    row_recv,
    side_send,
    side_recv,
    part_send,
    part_recv,
):
    group = lax.axis_index("groups")
    me = lax.axis_index("ep")
    lane = lax.axis_index("hg")
    rows, width = tokens_ref.shape
    _, chunks, half, chunk = gate_buf.shape
    shard = chunks * chunk
    pieces, _, _, _, piece = outgoing.shape
    batch = 16 // rows

    barrier = pltpu.get_barrier_semaphore()
    for r in range(n_hg):
        side = (lane + r) % n_hg

        def greet(d):
            peer = (me + d + (r == 0)) % n_ep
            pl.semaphore_signal(barrier, inc=1, device_id=(group, peer, side), device_id_type=MESH)

        loop(n_ep - (r == 0), greet)

    own = pltpu.make_async_copy(tokens_ref, tokens, own_sem.at[0])
    own.start()
    gain_copy = pltpu.make_async_copy(gain_ref, gain.at[0], own_sem.at[1])
    gain_copy.start()

    def first_copy(source, target, sem, r, c):
        k = pl.ds(pl.multiple_of((lane + r) % n_hg * half, 256), half)
        cols = pl.ds(pl.multiple_of(c * chunk, 128), chunk)
        return pltpu.make_async_copy(source.at[k, cols], target.at[r, c], sem.at[r, c])

    def gate_copy(r, c):
        return first_copy(gate_ref, gate_buf, gate_sem, r, c)

    def up_copy(r, c):
        return first_copy(up_ref, up_buf, up_sem, r, c)

    def down_copy(p, r):
        start = (lane + r) % n_hg * half + p * piece
        cols = pl.ds(pl.multiple_of(start, 128), piece)
        return pltpu.make_async_copy(down_ref.at[:, cols], down_buf.at[p, r], down_sem.at[p, r])

    for r in range(n_hg):

        def start_first(c):
            gate_copy(r, c).start()
            up_copy(r, c).start()

        loop(chunks, start_first)

    def start_down(p):
        for r in reversed(range(n_hg)):
            down_copy(p, r).start()

    loop(pieces, start_down)

    own.wait()
    gain_copy.wait()
    own_half = pl.ds(pl.multiple_of(lane * half, 256), half)
    stats = tokens[...].astype(jnp.float32)
    scale = lax.rsqrt(jnp.mean(stats * stats, axis=1, keepdims=True) + NORM_EPS)
    stats = tokens[:, own_half].astype(jnp.float32)
    gathered[0, me] = (stats * scale * gain[:, own_half]).astype(jnp.bfloat16)

    scores = scores_ref[...]
    weights = ROUTE_SCALE * scores / jnp.sum(scores, axis=1, keepdims=True)
    chosen = ids_ref[...]

    def weigh(s):
        expert = s * shard // FF
        total = jnp.sum(jnp.where(chosen == expert, weights, 0.0), axis=1, keepdims=True)
        coef[s] = jnp.broadcast_to(total, (rows, 128))

    loop(n_ep * n_hg, weigh)

    pl.semaphore_wait(barrier, n_ep * n_hg - 1)

    def send_rows(d):
        pltpu.make_async_remote_copy(
            src_ref=gathered.at[0, me],
            dst_ref=gathered.at[0, me],
            send_sem=row_send,
            recv_sem=row_recv,
            device_id=(group, (me + d + 1) % n_ep, lane),
            device_id_type=MESH,
        ).start()

    loop(n_ep - 1, send_rows)
    others = gathered.at[0, pl.ds(0, n_ep - 1)]
    pltpu.make_async_copy(others, others, row_recv).wait()
    forwards = [
        pltpu.make_async_remote_copy(
            src_ref=gathered.at[0],
            dst_ref=gathered.at[r],
            send_sem=side_send.at[r - 1],
            recv_sem=side_recv.at[r - 1],
            device_id=(group, me, (lane + n_hg - r) % n_hg),
            device_id_type=MESH,
        )
        for r in range(1, n_hg)
    ]
    for forward in forwards:
        forward.start()

    for r in range(n_hg):
        if r > 0:
            forwards[r - 1].wait_recv()

        def lay(i):
            stacked = jnp.concatenate(
                [gathered[r, i * batch + b].astype(jnp.float32) for b in range(batch)], axis=0
            )
            normed[r, pl.ds(pl.multiple_of(i * 16, 16), 16), :] = stacked.astype(jnp.bfloat16)

        loop(n_ep // batch, lay)

        def first(c):
            gate_copy(r, c).wait()
            up_copy(r, c).wait()
            gate_val = jnp.dot(normed[r], gate_buf[r, c], preferred_element_type=jnp.float32)
            up_val = jnp.dot(normed[r], up_buf[r, c], preferred_element_type=jnp.float32)
            if r > 0:
                gate_val = gate_sum[c] + gate_val
                up_val = up_sum[c] + up_val
            if r < n_hg - 1:
                gate_sum[c] = gate_val
                up_sum[c] = up_val
            else:
                value = gate_val / (1.0 + jnp.exp(-gate_val)) * up_val
                cols = pl.ds(pl.multiple_of(c * chunk, 128), chunk)
                act[:, cols] = value.astype(jnp.bfloat16)

        loop(chunks, first)

    source = me * n_hg + lane

    def second(p):
        for r in reversed(range(n_hg)):
            side = (lane + r) % n_hg
            down_copy(p, r).wait()
            value = jnp.dot(act[...], down_buf[p, r], preferred_element_type=jnp.float32)
            for j in range(n_ep):
                outgoing[p, r, j] = value[j * rows : (j + 1) * rows].astype(jnp.bfloat16)

            def send(d):
                peer = (me + d + (r == 0)) % n_ep
                pltpu.make_async_remote_copy(
                    src_ref=outgoing.at[p, r, peer],
                    dst_ref=incoming.at[p, source],
                    send_sem=part_send.at[p, r],
                    recv_sem=part_recv.at[p],
                    device_id=(group, peer, side),
                    device_id_type=MESH,
                ).start()

            loop(n_ep - (r == 0), send)
            if r == 0:
                pltpu.make_async_copy(
                    outgoing.at[p, r, me], incoming.at[p, source], part_recv.at[p]
                ).start()

    loop(pieces, second)

    def finish(p):
        here = incoming.at[p]
        pltpu.make_async_copy(here, here, part_recv.at[p]).wait()
        start = pl.multiple_of(lane * half + p * piece, 128)
        resid = tokens[:, pl.ds(start, piece)].astype(jnp.float32)

        def add(s, total):
            weight = jnp.concatenate([coef[s]] * (piece // 128), axis=1)
            return total + weight * incoming[p, s].astype(jnp.float32)

        moe = lax.fori_loop(
            0, n_ep * n_hg, add, jnp.zeros((rows, piece), jnp.float32), unroll=min(16, n_ep * n_hg)
        )
        cols = pl.ds(pl.multiple_of(p * piece, 128), piece)
        out_ref[:, cols] = resid + moe

    loop(pieces, finish)

    pltpu.make_async_copy(others, others, row_send).wait()
    for forward in forwards:
        forward.wait_send()

    def drain(p):
        for r in range(n_hg):
            sent = outgoing.at[p, r, pl.ds(0, n_ep - (r == 0))]
            pltpu.make_async_copy(sent, sent, part_send.at[p, r]).wait()

    loop(pieces, drain)


def body(tokens, norm_gain, route_scores, expert_ids, gate_weight, up_weight, down_weight):
    n_ep = lax.axis_size("ep")
    n_hg = lax.axis_size("hg")
    rows, width = tokens.shape
    shard = gate_weight.shape[1]
    chunk = min(shard, 512)
    chunks = shard // chunk
    half = width // n_hg
    pieces = 2
    piece = half // pieces
    total = rows * n_ep
    sources = n_ep * n_hg
    hbm = pl.BlockSpec(memory_space=pl.ANY)
    vmem = pl.BlockSpec(memory_space=pltpu.VMEM)
    dma = pltpu.SemaphoreType.DMA
    mixed = pl.pallas_call(
        functools.partial(kernel, n_ep, n_hg),
        out_shape=jax.ShapeDtypeStruct((rows, half), jnp.float32),
        in_specs=[hbm, hbm, vmem, vmem, hbm, hbm, hbm],
        out_specs=vmem,
        scratch_shapes=[
            pltpu.VMEM((rows, width), jnp.bfloat16),
            pltpu.VMEM((1, width), jnp.float32),
            pltpu.VMEM((n_hg, n_ep, rows, half), jnp.bfloat16),
            pltpu.VMEM((n_hg, total, half), jnp.bfloat16),
            pltpu.VMEM((n_hg, chunks, half, chunk), jnp.bfloat16),
            pltpu.VMEM((n_hg, chunks, half, chunk), jnp.bfloat16),
            pltpu.VMEM((chunks, total, chunk), jnp.float32),
            pltpu.VMEM((chunks, total, chunk), jnp.float32),
            pltpu.VMEM((total, shard), jnp.bfloat16),
            pltpu.VMEM((pieces, n_hg, shard, piece), jnp.bfloat16),
            pltpu.VMEM((pieces, n_hg, n_ep, rows, piece), jnp.bfloat16),
            pltpu.VMEM((pieces, sources, rows, piece), jnp.bfloat16),
            pltpu.VMEM((sources, rows, 128), jnp.float32),
            dma((n_hg, chunks)),
            dma((n_hg, chunks)),
            dma((pieces, n_hg)),
            dma((2,)),
            dma,
            dma,
            dma((n_hg - 1,)),
            dma((n_hg - 1,)),
            dma((pieces, n_hg)),
            dma((pieces,)),
        ],
        compiler_params=pltpu.CompilerParams(
            collective_id=0, has_side_effects=True, vmem_limit_bytes=56 * 1024 * 1024
        ),
    )(tokens, norm_gain, route_scores, expert_ids, gate_weight, up_weight, down_weight)
    return mixed.astype(jnp.bfloat16)


def solution(mesh):
    return jax.shard_map(
        body,
        mesh=mesh,
        in_specs=(
            P(("groups", "ep"), None),
            P(),
            P(("groups", "ep"), None),
            P(("groups", "ep"), None),
            P(None, ("ep", "hg")),
            P(None, ("ep", "hg")),
            P(("ep", "hg"), None),
        ),
        out_specs=P(("groups", "ep"), "hg"),
        check_vma=False,
    )
```

time: 34.9 us -> 27.7 us (0.79)
  Pallas kernels: 31.9 us -> 26.2 us
  local copies, waits for them, and re-layouts: 2.65 us -> 0 us
  other arithmetic: 0 us -> 1.35 us
    pallas_call x1, Pallas kernels: 31.9 us -> 26.2 us  [body(): pl.pallas_call(functools.partial(kernel, n_ep, n_hg), out_shape=jax.Shape...]
    convert_element_type x0 -> x1, other arithmetic: none -> 1.35 us  [body(): return mixed.astype(jnp.bfloat16)]
    reshape x1 -> x0, local copies, waits for them, and re-layouts: 1.33 us -> none  [body(): norm_gain.reshape(1, width)]
    unnamed x1 -> x0, local copies, waits for them, and re-layouts: 1.32 us -> none
where the time goes in v2:
time: 27.7 us; the launch traced here: 27.6 us
  Pallas kernels  26.2 us (95%)
  other arithmetic  1.35 us (5%)
    pallas_call x1, Pallas kernels, body(): pl.pallas_call(functools.partial(kernel, n_ep, n_hg), out_shape=jax.Shape...  26.2 us
    convert_element_type x1, other arithmetic, body(): return mixed.astype(jnp.bfloat16)  1.35 us

profile of v2, /device:TPU:0, one launch (start us, length us, event | category | flops | bytes accessed | tf_op | source)
XLA Modules:
  0.0 27.6 jit_solution(7226369841115717580)
XLA Ops:
  0.0 26.2 %shard_map.73 = f32[4,1792]{1,0:T(4,128)} custom-call(bf16[4,3584]{1,0:T(4,128)(2,1)} %tokens_ref.1, f32[3584]{0:T(1024)} %gain_ref.1, f32[4,8]{1,0:T(4,128)} %scores_ref.1, s32[4,8]{1,0:T(4,128)} %ids_ref.1, bf16[3584,2048]{1,0:T(8,128)(2,1)} %gate_ref.1, bf16[3584,2048]{1,0:T(8,128)(2,1)} %up_ref.1, bf16[2048,3584]{1,0:T(8,128)(2,1)} %down_ref.1), custom_call_target="tpu_custom_call" | custom-call | tf_op jit(solution)/shard_map/pallas_call | solution.py:268
  26.2 1.4 %convert_element_type.3 = bf16[4,1792]{1,0:T(4,128)(2,1)} convert(f32[4,1792]{1,0:T(4,128)} %shard_map.73) | non-fusion elementwise | flops 7168 | bytes 43008 | tf_op jit(solution)/shard_map/convert_element_type | solution.py:302

commit v3 on v2

--- a/solution.py
+++ b/solution.py
@@ -45,6 +45,8 @@
     up_sum,
     act,
     down_buf,
+    hand_out,
+    hand_in,
     outgoing,
     incoming,
     coef,
@@ -56,6 +58,10 @@
     row_recv,
     side_send,
     side_recv,
+    coef_send,
+    coef_recv,
+    hand_send,
+    hand_recv,
     part_send,
     part_recv,
 ):
@@ -65,18 +71,19 @@
     rows, width = tokens_ref.shape
     _, chunks, half, chunk = gate_buf.shape
     shard = chunks * chunk
-    pieces, _, _, _, piece = outgoing.shape
+    pieces, _, _, piece = outgoing.shape
     batch = 16 // rows
 
     barrier = pltpu.get_barrier_semaphore()
-    for r in range(n_hg):
+
+    def greet(d):
+        peer = (me + d + 1) % n_ep
+        pl.semaphore_signal(barrier, inc=1, device_id=(group, peer, lane), device_id_type=MESH)
+
+    loop(n_ep - 1, greet)
+    for r in range(1, n_hg):
         side = (lane + r) % n_hg
-
-        def greet(d):
-            peer = (me + d + (r == 0)) % n_ep
-            pl.semaphore_signal(barrier, inc=1, device_id=(group, peer, side), device_id_type=MESH)
-
-        loop(n_ep - (r == 0), greet)
+        pl.semaphore_signal(barrier, inc=1, device_id=(group, me, side), device_id_type=MESH)
 
     own = pltpu.make_async_copy(tokens_ref, tokens, own_sem.at[0])
     own.start()
@@ -107,11 +114,8 @@
 
         loop(chunks, start_first)
 
-    def start_down(p):
-        for r in reversed(range(n_hg)):
-            down_copy(p, r).start()
-
-    loop(pieces, start_down)
+    for r in reversed(range(n_hg)):
+        loop(pieces, lambda p: down_copy(p, r).start())
 
     own.wait()
     gain_copy.wait()
@@ -125,14 +129,13 @@
     weights = ROUTE_SCALE * scores / jnp.sum(scores, axis=1, keepdims=True)
     chosen = ids_ref[...]
 
-    def weigh(s):
-        expert = s * shard // FF
-        total = jnp.sum(jnp.where(chosen == expert, weights, 0.0), axis=1, keepdims=True)
-        coef[s] = jnp.broadcast_to(total, (rows, 128))
-
-    loop(n_ep * n_hg, weigh)
-
-    pl.semaphore_wait(barrier, n_ep * n_hg - 1)
+    expert = lax.broadcasted_iota(jnp.int32, (rows, 128), 1)
+    total = jnp.zeros((rows, 128), jnp.float32)
+    for k in range(scores.shape[1]):
+        total = total + jnp.where(chosen[:, k : k + 1] == expert, weights[:, k : k + 1], 0.0)
+    coef[me] = total
+
+    pl.semaphore_wait(barrier, n_ep + n_hg - 2)
 
     def send_rows(d):
         pltpu.make_async_remote_copy(
@@ -145,6 +148,18 @@
         ).start()
 
     loop(n_ep - 1, send_rows)
+
+    def send_coef(d):
+        pltpu.make_async_remote_copy(
+            src_ref=coef.at[me],
+            dst_ref=coef.at[me],
+            send_sem=coef_send,
+            recv_sem=coef_recv,
+            device_id=(group, (me + d + 1) % n_ep, lane),
+            device_id_type=MESH,
+        ).start()
+
+    loop(n_ep - 1, send_coef)
     others = gathered.at[0, pl.ds(0, n_ep - 1)]
     pltpu.make_async_copy(others, others, row_recv).wait()
     forwards = [
@@ -191,50 +206,71 @@
 
         loop(chunks, first)
 
-    source = me * n_hg + lane
-
-    def second(p):
-        for r in reversed(range(n_hg)):
-            side = (lane + r) % n_hg
-            down_copy(p, r).wait()
-            value = jnp.dot(act[...], down_buf[p, r], preferred_element_type=jnp.float32)
-            for j in range(n_ep):
-                outgoing[p, r, j] = value[j * rows : (j + 1) * rows].astype(jnp.bfloat16)
-
-            def send(d):
-                peer = (me + d + (r == 0)) % n_ep
-                pltpu.make_async_remote_copy(
-                    src_ref=outgoing.at[p, r, peer],
-                    dst_ref=incoming.at[p, source],
-                    send_sem=part_send.at[p, r],
-                    recv_sem=part_recv.at[p],
-                    device_id=(group, peer, side),
-                    device_id_type=MESH,
-                ).start()
-
-            loop(n_ep - (r == 0), send)
-            if r == 0:
-                pltpu.make_async_copy(
-                    outgoing.at[p, r, me], incoming.at[p, source], part_recv.at[p]
-                ).start()
-
-    loop(pieces, second)
+    other_coefs = coef.at[pl.ds(0, n_ep - 1)]
+    pltpu.make_async_copy(other_coefs, other_coefs, coef_recv).wait()
+    held = (me * n_hg + lane) * shard // FF
+    column = lax.broadcasted_iota(jnp.int32, (rows * n_ep, 128), 1)
+    every = jnp.concatenate([coef[j] for j in range(n_ep)], axis=0)
+    weight = jnp.sum(jnp.where(column == held, every, 0.0), axis=1, keepdims=True)
+
+    def second(p, r):
+        down_copy(p, r).wait()
+        return weight * jnp.dot(act[...], down_buf[p, r], preferred_element_type=jnp.float32)
+
+    def hand(p, r):
+        return pltpu.make_async_remote_copy(
+            src_ref=hand_out.at[p, r - 1],
+            dst_ref=hand_in.at[p, r - 1],
+            send_sem=hand_send.at[p, r - 1],
+            recv_sem=hand_recv.at[p, r - 1],
+            device_id=(group, me, (lane + r) % n_hg),
+            device_id_type=MESH,
+        )
+
+    for r in range(1, n_hg):
+
+        def give(p):
+            hand_out[p, r - 1] = second(p, r).astype(jnp.bfloat16)
+            hand(p, r).start()
+
+        loop(pieces, give)
+
+    def send_back(p):
+        value = second(p, 0)
+        for r in range(1, n_hg):
+            hand(p, r).wait_recv()
+            value = value + hand_in[p, r - 1].astype(jnp.float32)
+        for j in range(n_ep):
+            outgoing[p, j] = value[j * rows : (j + 1) * rows].astype(jnp.bfloat16)
+
+        def send(d):
+            peer = (me + d + 1) % n_ep
+            pltpu.make_async_remote_copy(
+                src_ref=outgoing.at[p, peer],
+                dst_ref=incoming.at[p, me],
+                send_sem=part_send.at[p],
+                recv_sem=part_recv.at[p],
+                device_id=(group, peer, lane),
+                device_id_type=MESH,
+            ).start()
+
+        loop(n_ep - 1, send)
+        pltpu.make_async_copy(outgoing.at[p, me], incoming.at[p, me], part_recv.at[p]).start()
+
+    loop(pieces, send_back)
 
     def finish(p):
         here = incoming.at[p]
         pltpu.make_async_copy(here, here, part_recv.at[p]).wait()
         start = pl.multiple_of(lane * half + p * piece, 128)
-        resid = tokens[:, pl.ds(start, piece)].astype(jnp.float32)
+        total = tokens[:, pl.ds(start, piece)].astype(jnp.float32)
 
         def add(s, total):
-            weight = jnp.concatenate([coef[s]] * (piece // 128), axis=1)
-            return total + weight * incoming[p, s].astype(jnp.float32)
-
-        moe = lax.fori_loop(
-            0, n_ep * n_hg, add, jnp.zeros((rows, piece), jnp.float32), unroll=min(16, n_ep * n_hg)
-        )
+            return total + incoming[p, s].astype(jnp.float32)
+
+        total = lax.fori_loop(0, n_ep, add, total, unroll=min(8, n_ep))
         cols = pl.ds(pl.multiple_of(p * piece, 128), piece)
-        out_ref[:, cols] = resid + moe
+        out_ref[:, cols] = total
 
     loop(pieces, finish)
 
@@ -242,10 +278,13 @@
     for forward in forwards:
         forward.wait_send()
 
+    pltpu.make_async_copy(other_coefs, other_coefs, coef_send).wait()
+
     def drain(p):
-        for r in range(n_hg):
-            sent = outgoing.at[p, r, pl.ds(0, n_ep - (r == 0))]
-            pltpu.make_async_copy(sent, sent, part_send.at[p, r]).wait()
+        for r in range(1, n_hg):
+            hand(p, r).wait_send()
+        sent = outgoing.at[p, pl.ds(0, n_ep - 1)]
+        pltpu.make_async_copy(sent, sent, part_send.at[p]).wait()
 
     loop(pieces, drain)
 
@@ -261,13 +300,12 @@
     pieces = 2
     piece = half // pieces
     total = rows * n_ep
-    sources = n_ep * n_hg
     hbm = pl.BlockSpec(memory_space=pl.ANY)
     vmem = pl.BlockSpec(memory_space=pltpu.VMEM)
     dma = pltpu.SemaphoreType.DMA
     mixed = pl.pallas_call(
         functools.partial(kernel, n_ep, n_hg),
-        out_shape=jax.ShapeDtypeStruct((rows, half), jnp.float32),
+        out_shape=pltpu.VMEM((rows, half), jnp.float32),
         in_specs=[hbm, hbm, vmem, vmem, hbm, hbm, hbm],
         out_specs=vmem,
         scratch_shapes=[
@@ -281,9 +319,11 @@
             pltpu.VMEM((chunks, total, chunk), jnp.float32),
             pltpu.VMEM((total, shard), jnp.bfloat16),
             pltpu.VMEM((pieces, n_hg, shard, piece), jnp.bfloat16),
-            pltpu.VMEM((pieces, n_hg, n_ep, rows, piece), jnp.bfloat16),
-            pltpu.VMEM((pieces, sources, rows, piece), jnp.bfloat16),
-            pltpu.VMEM((sources, rows, 128), jnp.float32),
+            pltpu.VMEM((pieces, n_hg - 1, total, piece), jnp.bfloat16),
+            pltpu.VMEM((pieces, n_hg - 1, total, piece), jnp.bfloat16),
+            pltpu.VMEM((pieces, n_ep, rows, piece), jnp.bfloat16),
+            pltpu.VMEM((pieces, n_ep, rows, piece), jnp.bfloat16),
+            pltpu.VMEM((n_ep, rows, 128), jnp.float32),
             dma((n_hg, chunks)),
             dma((n_hg, chunks)),
             dma((pieces, n_hg)),
@@ -292,7 +332,11 @@
             dma,
             dma((n_hg - 1,)),
             dma((n_hg - 1,)),
-            dma((pieces, n_hg)),
+            dma,
+            dma,
+            dma((pieces, n_hg - 1)),
+            dma((pieces, n_hg - 1)),
+            dma((pieces,)),
             dma((pieces,)),
         ],
         compiler_params=pltpu.CompilerParams(

time: 27.7 us -> 25.9 us (0.935)
  Pallas kernels: 26.2 us -> 25.1 us
  other arithmetic: 1.35 us -> 0.61 us
    pallas_call x1, Pallas kernels: 26.2 us -> 25.1 us  [body(): pl.pallas_call(functools.partial(kernel, n_ep, n_hg), out_shape=pltpu.VME...]
    convert_element_type x1, other arithmetic: 1.35 us -> 0.61 us  [body(): return mixed.astype(jnp.bfloat16)]
where the time goes in v3:
time: 25.9 us; the launch traced here: 25.7 us
  Pallas kernels  25.1 us (97%)
  other arithmetic  0.61 us (2%)
    pallas_call x1, Pallas kernels, body(): pl.pallas_call(functools.partial(kernel, n_ep, n_hg), out_shape=pltpu.VME...  25.1 us
    convert_element_type x1, other arithmetic, body(): return mixed.astype(jnp.bfloat16)  0.61 us

profile of v3, /device:TPU:0, one launch (start us, length us, event | category | flops | bytes accessed | tf_op | source)
XLA Modules:
  0.0 25.7 jit_solution(18396005890661894931)
XLA Ops:
  0.0 25.1 %shard_map.73 = f32[4,1792]{1,0:T(4,128)S(1)} custom-call(bf16[4,3584]{1,0:T(4,128)(2,1)} %tokens_ref.1, f32[3584]{0:T(1024)} %gain_ref.1, f32[4,8]{1,0:T(4,128)} %scores_ref.1, s32[4,8]{1,0:T(4,128)} %ids_ref.1, bf16[3584,2048]{1,0:T(8,128)(2,1)} %gate_ref.1, bf16[3584,2048]{1,0:T(8,128)(2,1)} %up_ref.1, bf16[2048,3584]{1,0:T(8,128)(2,1)} %down_ref.1), custom_call_target="tpu_custom_call" | custom-call | tf_op jit(solution)/shard_map/pallas_call | solution.py:306
  25.1 0.6 %convert_element_type.3 = bf16[4,1792]{1,0:T(4,128)(2,1)} convert(f32[4,1792]{1,0:T(4,128)S(1)} %shard_map.73) | non-fusion elementwise | flops 7168 | bytes 43008 | tf_op jit(solution)/shard_map/convert_element_type | solution.py:346
